TPU v7x, 32 devices: a whole 2x2x4 slice. The times are simulated.
32 devices in a mesh: node: 8 (over y, x, core), tm: 4 (over z).
Axes of the slice: x: 2, y: 2, z: 4, core: 2. Of those that a mesh axis runs over, the one named last changes fastest.
Arguments:
- observed: bfloat16 [32768, 4096], P('node', 'tm'), may hold values from 0.5 to 32
- node_factor: bfloat16 [64, 32768], P(None, ('node', 'tm')), may hold values from 0.19921875 to 1
- time_factor: bfloat16 [64, 256], P(None, 'tm'), may hold values from 0.19921875 to 1
- species_factor: bfloat16 [64, 16], replicated, may hold values from 0.19921875 to 1
Outputs:
- grad_node: float32 [64, 32768], P(None, ('node', 'tm'))
- grad_time: float32 [64, 256], P(None, 'tm')
- grad_species: float32 [64, 16], replicated
All inputs are finite; a program needn't handle non-finite values.
Results may differ from a plain program's by a relative error of at most 0.0017.
Values may be sent and summed in bfloat16 or wider, within the bound.
A program may use at most 64 MiB of HBM per device.

v0:
```python
import math

import jax
import jax.numpy as jnp
from jax import lax
from jax.sharding import PartitionSpec as P


def widen(values):
    return lax.optimization_barrier(values).astype(jnp.float32)


def shards(observed, node_factor, time_factor, species_factor):
    factor_rank = node_factor.shape[0]
    time_vals = time_factor.astype(jnp.float32)
    species_vals = species_factor.astype(jnp.float32)
    time_dev = time_vals.shape[1]
    species = species_vals.shape[1]
    node_rows = observed.shape[0]
    flat_width = observed.shape[1]
    khatri = (
        (time_vals[:, :, None] * species_vals[:, None, :])
        .reshape(factor_rank, flat_width)
        .astype(jnp.bfloat16)
    )
    khatri_wide = widen(khatri)
    factor_wide = lax.all_gather(node_factor, "tm", axis=1, tiled=True).astype(jnp.float32)
    modelled = lax.dot_general(
        factor_wide, khatri_wide, (((0,), (0,)), ((), ())), precision=lax.Precision.HIGHEST
    )
    derivative = ((modelled - observed.astype(jnp.float32)) / (modelled * modelled)).astype(
        jnp.bfloat16
    )
    derivative_wide = widen(derivative)
    node_part = lax.dot_general(
        khatri_wide, derivative_wide, (((1,), (1,)), ((), ())), precision=lax.Precision.HIGHEST
    )
    node_grads = node_part
    contracted = lax.dot_general(
        derivative_wide, factor_wide, (((0,), (1,)), ((), ())), precision=lax.Precision.HIGHEST
    )
    node_grads, contracted = (node_grads, contracted)
    tm_count = lax.axis_size("tm")
    steps_all = time_dev * tm_count
    nodes_all = node_rows * lax.axis_size("node")
    grad_node = lax.psum_scatter(node_grads, "tm", scatter_dimension=1, tiled=True)
    grad_node = grad_node / math.sqrt(steps_all * species)
    by_step = contracted.reshape(time_dev, species, factor_rank)
    time_grad = jnp.einsum("tsr,rs->rt", by_step, species_vals, precision=lax.Precision.HIGHEST)
    species_grad = jnp.einsum("tsr,rt->rs", by_step, time_vals, precision=lax.Precision.HIGHEST)
    time_grad = lax.psum(time_grad, "node")
    species_grad = lax.psum(species_grad, ("node", "tm"))
    grad_time = time_grad / math.sqrt(nodes_all * species)
    grad_species = species_grad / math.sqrt(nodes_all * steps_all)
    return (grad_node, grad_time, grad_species)


def solution(mesh):
    in_specs = (P("node", "tm"), P(None, ("node", "tm")), P(None, "tm"), P())
    out_specs = (P(None, ("node", "tm")), P(None, "tm"), P())
    return jax.shard_map(shards, mesh=mesh, in_specs=in_specs, out_specs=out_specs, check_vma=False)
```

profile of v0, /device:TPU:0, one launch (start us, length us, event | category | flops | bytes accessed | tf_op | source)
XLA Modules:
  0.0 129.4 jit_solution(14586235946840164610)
XLA Ops:
  7.2 0.0 reduce-scatter.2.cloned.1.call-start
  7.2 0.8 copy.9
  8.0 0.7 convert_element_type.22
  8.7 0.1 multiply_convert_fusion
  8.8 17.6 %all_gather.3 = bf16[64,4096]{1,0:T(8,128)(2,1)S(1)} all-gather(bf16[64,1024]{1,0:T(8,128)(2,1)} %param.5), channel_id=1, replica_groups=mesh['node'=8,'tm'=4] {'tm'}, dimensions={1}, use_global_device_ids=true | all-gather | bytes 655360 | tf_op jit(solution)/shard_map/all_gather | solution.py:27
  26.3 11.3 %copy.10 = bf16[4096,1024]{0,1:T(8,128)(2,1)} copy(bf16[4096,1024]{1,0:T(8,128)(2,1)} %param.4) | data formatting | bytes 16777216 | tf_op args[0]
  37.6 5.6 %fusion.1 = bf16[4096,1024]{0,1:T(8,128)(2,1)S(1)} fusion(bf16[4096,1024]{0,1:T(8,128)(2,1)} %copy.10, bf16[64,1024]{0,1:T(8,128)(2,1)S(1)} %bitcast.23, bf16[64,4096]{1,0:T(8,128)(2,1)S(1)} %all_gather.3), kind=kOutput, calls=%fused_computation.3 | convolution fusion | flops 557842432 | bytes 17432576 | tf_op jit(solution)/shard_map/dot_general | solution.py:28
  43.2 0.0 copy-start
  43.2 3.2 %copy-done = bf16[4096,1024]{0,1:T(8,128)(2,1)} copy-done((bf16[4096,1024]{0,1:T(8,128)(2,1)}, bf16[4096,1024]{0,1:T(8,128)(2,1)S(1)}, u32[]{:S(2)}) %copy-start) | copy-done | bytes 8388632
  46.4 2.7 %fusion.2 = f32[64,4096]{1,0:T(8,128)} fusion(bf16[64,1024]{0,1:T(8,128)(2,1)S(1)} %bitcast.24, bf16[4096,1024]{0,1:T(8,128)(2,1)S(1)} %fusion.1), kind=kOutput, calls=%fused_computation.10 | convolution fusion | flops 536870912 | bytes 9568256 | tf_op jit(solution)/shard_map/dot_general | solution.py:35
  49.1 0.0 reduce-scatter.2.cloned.1.call-update
  49.1 5.7 %multiply_reduce_fusion.1 = (f32[64,64]{0,1:T(8,128)S(1)}, f32[1024,64]{1,0:T(8,128)S(1)}) fusion(f32[64,16]{0,1:T(8,128)S(1)} %convert_element_type.22, bf16[4096,1024]{0,1:T(8,128)(2,1)} %copy-done, bf16[64,4096]{1,0:T(8,128)(2,1)S(1)} %all_gather.3), kind=kOutput, calls=%fused_computation.5 | convolution fusion | flops 536997888 | bytes 9195520 | tf_op jit(solution)/shard_map/dot_general | solution.py:39
  54.9 0.1 copy.18
  54.9 0.1 multiply_reduce_fusion
  55.0 41.5 %psum.15 = f32[64,16]{0,1:T(8,128)S(1)} all-reduce(f32[64,16]{0,1:T(8,128)S(1)} %multiply_reduce_fusion), channel_id=1, replica_groups=mesh['node'=8,'tm'=4] {'node','tm'}, use_global_device_ids=true, to_apply=%region_2.0 | all-reduce | flops 1024 | bytes 8192 | tf_op jit(solution)/shard_map/psum | solution.py:52
  96.5 23.1 %psum.14 = f32[64,64]{1,0:T(8,128)S(1)} all-reduce(f32[64,64]{1,0:T(8,128)S(1)} %copy.18), channel_id=1, replica_groups=mesh['node'=8,'tm'=4] {'node'}, use_global_device_ids=true, to_apply=%region_1.0 | all-reduce | flops 4096 | bytes 32768 | tf_op jit(solution)/shard_map/psum | solution.py:51
  119.6 0.6 broadcast_multiply_fusion.2
  120.2 0.6 broadcast_multiply_fusion.1
  120.8 0.0 reduce-scatter.2.cloned.1.call-done
  120.8 1.7 %broadcast_multiply_fusion = f32[64,1024]{1,0:T(8,128)} fusion(f32[64,1024]{1,0:T(8,128)} %reduce-scatter.2.cloned.1.call-done), kind=kLoop, calls=%fused_computation.7 | loop fusion | flops 65536 | bytes 524288 | tf_op jit(solution)/shard_map/div | solution.py:47
Async XLA Ops:
  7.2 113.7 %reduce-scatter.2.cloned.1.call-start = ((), (), s32[]{:S(2)}) async-start(), calls=%async_computation.1 | async-start | bytes 1310720 | tf_op jit(solution)/shard_map/reduce_scatter | solution.py:46
  43.2 3.2 %copy-start = (bf16[4096,1024]{0,1:T(8,128)(2,1)}, bf16[4096,1024]{0,1:T(8,128)(2,1)S(1)}, u32[]{:S(2)}) copy-start(bf16[4096,1024]{0,1:T(8,128)(2,1)S(1)} %fusion.1) | copy-start | bytes 25165828
Sparse Core Ops, SparseCore 0:
  49.3 29.1 reduce-scatter.1
where the time goes:
time: 130 us; the launch traced here: 129 us
  blocking collectives  82.1 us (63%)
  local copies, waits for them, and re-layouts  15.3 us (12%)
  between operations  14.1 us (11%)
  matrix products  14 us (11%)
  other arithmetic  3.76 us (3%)
    psum x1, blocking collectives, shards(): species_grad = lax.psum(species_grad, ('node', 'tm'))  41.5 us
    psum x1, blocking collectives, shards(): time_grad = lax.psum(time_grad, 'node')  23.1 us
    all_gather x1, blocking collectives, shards(): lax.all_gather(node_factor, 'tm', axis=1, tiled=True).astype(jnp.float32)  17.6 us
    unnamed x3, local copies, waits for them, and re-layouts  14.5 us
    dot_general x1, matrix products, shards(): lax.dot_general(derivative_wide, factor_wide, (((0,), (1,)), ((), ())), p...  5.7 us
    dot_general x1, matrix products, shards(): lax.dot_general(factor_wide, khatri_wide, (((0,), (0,)), ((), ())), preci...  5.63 us
    dot_general x1, matrix products, shards(): lax.dot_general(khatri_wide, derivative_wide, (((1,), (1,)), ((), ())), p...  2.68 us
  transfers between devices with their start and end apart: 1, of which 0 were waited for; matrix products, arithmetic and copies ran while one was open for 5% of the time, Pallas kernels for 0%

commit v1 on v0

v1 whole, which is shorter than its diff:
```python
import functools
import math

import jax
import jax.numpy as jnp
from jax import lax
from jax.experimental import pallas as pl
from jax.experimental.pallas import tpu as pltpu
from jax.sharding import PartitionSpec as P

MESH = pl.DeviceIdType.MESH
F32 = jnp.float32
BF16 = jnp.bfloat16
LINK = jnp.float32
LOOK = 2
COLS = 256


def kernel(
    nodes_n, tm_n, width, scales,
    obs_ref, nf_ref, tf_ref, sf_ref,
    gnode_ref, gtime_ref, gspec_ref,
    obs_v, gath, mine, out, above, below, khatri, spread_t, spread_s, ctot,
    small, small_in, spec_out, spec_in,
    obs_sem, g_send, g_recv, r_send, a_recv, b_recv, s_send, s_recv, p_send, p_recv,
):
    rank, own = nf_ref.shape
    rows, flat = obs_ref.shape
    steps = tf_ref.shape[1]
    species = sf_ref.shape[1]
    per = own // width
    total = tm_n * per
    lanes = small.shape[1]
    z = lax.axis_index("tm")
    me = lax.axis_index("node")
    top = tm_n - 1
    scale_node, scale_time, scale_spec = scales

    def place(p):
        low = jnp.minimum(z, top - z)
        q = p - per
        k = q // (2 * per) + 1
        w = q % (2 * per)
        pair_owner = jnp.where(w % 2 == 0, z - k, z + k)
        q2 = q - 2 * low * per
        dist = low + 1 + q2 // per
        far_owner = jnp.where(z < top - z, z + dist, z - dist)
        paired = q2 < 0
        owner = jnp.where(p < per, z, jnp.where(paired, pair_owner, far_owner))
        chunk = jnp.where(p < per, p, jnp.where(paired, w // 2, q2 % per))
        return owner, owner * per + chunk

    def obs_copy(g):
        at = pl.ds(pl.multiple_of(g * width, width), width)
        return pltpu.make_async_copy(obs_ref.at[at, :], obs_v.at[at, :], obs_sem.at[g])

    def start_obs(p, _):
        obs_copy(place(p)[1]).start()
        return 0

    def gather_copy(g, up):
        return pltpu.make_async_remote_copy(
            src_ref=gath.at[g], dst_ref=gath.at[g],
            send_sem=g_send.at[1 if up else 0, g], recv_sem=g_recv.at[g],
            device_id={"tm": z + 1 if up else z - 1}, device_id_type=MESH,
        )

    def sum_copy(g, up):
        return pltpu.make_async_remote_copy(
            src_ref=out.at[g], dst_ref=(below if up else above).at[g],
            send_sem=r_send.at[g], recv_sem=(b_recv if up else a_recv).at[g],
            device_id={"tm": z + 1 if up else z - 1}, device_id_type=MESH,
        )

    def small_copy(k):
        return pltpu.make_async_remote_copy(
            src_ref=small, dst_ref=small_in.at[k - 1],
            send_sem=s_send.at[k - 1], recv_sem=s_recv.at[k - 1],
            device_id={"node": lax.rem(me + k, nodes_n)}, device_id_type=MESH,
        )

    def spec_copy(k):
        return pltpu.make_async_remote_copy(
            src_ref=spec_out, dst_ref=spec_in.at[k - 1],
            send_sem=p_send.at[k - 1], recv_sem=p_recv.at[k - 1],
            device_id={"tm": lax.rem(z + k, tm_n)}, device_id_type=MESH,
        )

    barrier = pltpu.get_barrier_semaphore()
    for k in range(1, nodes_n):
        pl.semaphore_signal(
            barrier, inc=1, device_id={"node": lax.rem(me + k, nodes_n)}, device_id_type=MESH
        )
    for k in range(1, tm_n):
        pl.semaphore_signal(
            barrier, inc=1, device_id={"tm": lax.rem(z + k, tm_n)}, device_id_type=MESH
        )
    lax.fori_loop(0, total, start_obs, 0)
    for c in range(per):
        gath[z * per + c] = nf_ref[:, c * width:(c + 1) * width]
    pl.semaphore_wait(barrier, nodes_n - 1 + tm_n - 1)

    def start_gather(c, _):
        g = z * per + c

        @pl.when(z < top)
        def _():
            gather_copy(g, True).start()

        @pl.when(z > 0)
        def _():
            gather_copy(g, False).start()

        return 0

    lax.fori_loop(0, per, start_gather, 0)

    col = lax.broadcasted_iota(jnp.int32, (steps, flat), 1)
    row = lax.broadcasted_iota(jnp.int32, (steps, flat), 0) * species
    wide_t = jnp.where((col >= row) & (col < row + species), 1.0, 0.0).astype(BF16)
    col_s = lax.rem(lax.broadcasted_iota(jnp.int32, (species, flat), 1), species)
    row_s = lax.broadcasted_iota(jnp.int32, (species, flat), 0)
    wide_s = jnp.where(col_s == row_s, 1.0, 0.0).astype(BF16)
    spread_t[...] = jnp.dot(tf_ref[...], wide_t, preferred_element_type=F32)
    spread_s[...] = jnp.dot(sf_ref[...], wide_s, preferred_element_type=F32)
    khatri[...] = (spread_t[...] * spread_s[...]).astype(BF16)
    ctot[...] = jnp.zeros_like(ctot)

    def relay(p):
        owner, g = place(p)

        @pl.when(owner != z)
        def _():
            gather_copy(g, True).wait_recv()

        @pl.when((owner < z) & (z < top))
        def _():
            gather_copy(g, True).start()

        @pl.when((owner > z) & (z > 0))
        def _():
            gather_copy(g, False).start()

    def compute(g):
        obs_copy(g).wait()
        factor = gath[g]
        at = pl.ds(pl.multiple_of(g * width, width), width)
        part = jnp.zeros((rank, width), F32)
        for c in range(0, flat, COLS):
            kh = khatri[:, c:c + COLS]
            modelled = lax.dot_general(
                factor, kh, (((0,), (0,)), ((), ())), preferred_element_type=F32
            )
            gap = modelled - obs_v[at, c:c + COLS].astype(F32)
            derivative = (gap / (modelled * modelled)).astype(BF16)
            part = part + lax.dot_general(
                kh, derivative, (((1,), (1,)), ((), ())), preferred_element_type=F32
            )
            ctot[:, c:c + COLS] += jnp.dot(factor, derivative, preferred_element_type=F32)
        return part

    def step(p, _):
        @pl.when(p + LOOK < total)
        def _():
            relay(p + LOOK)

        owner, g = place(p)
        part = compute(g)
        mine[g] = part

        @pl.when((z == top) & (owner < z))
        def _():
            out[g] = part.astype(out.dtype)
            sum_copy(g, False).start()

        @pl.when((z == 0) & (owner > z))
        def _():
            out[g] = part.astype(out.dtype)
            sum_copy(g, True).start()

        return 0

    for p in range(LOOK):
        relay(p)
    lax.fori_loop(0, total, step, 0)

    time_col = lax.broadcasted_iota(jnp.int32, (flat, lanes), 1)
    time_row = lax.broadcasted_iota(jnp.int32, (flat, lanes), 0)
    at_step = time_col * species
    pick_t = jnp.where((time_row >= at_step) & (time_row < at_step + species), 1.0, 0.0)
    pick_s = jnp.where(lax.rem(time_row, species) == time_col - steps, 1.0, 0.0)
    small[...] = jnp.dot(
        ctot[...] * spread_s[...], pick_t, precision=lax.Precision.HIGHEST,
        preferred_element_type=F32,
    ) + jnp.dot(
        ctot[...] * spread_t[...], pick_s, precision=lax.Precision.HIGHEST,
        preferred_element_type=F32,
    )
    for k in range(1, nodes_n):
        small_copy(k).start()

    def pass_up(g, _):
        sum_copy(g, True).wait_recv()
        out[g] = (mine[g] + below[g].astype(F32)).astype(out.dtype)
        sum_copy(g, True).start()
        return 0

    def pass_down(g, _):
        sum_copy(g, False).wait_recv()
        out[g] = (mine[g] + above[g].astype(F32)).astype(out.dtype)
        sum_copy(g, False).start()
        return 0

    def all_down():
        def owner_down(i, _):
            first = (z - 1 - i) * per
            return lax.fori_loop(first, first + per, pass_down, 0)

        lax.fori_loop(0, z, owner_down, 0)

    def all_up():
        lax.fori_loop((z + 1) * per, total, pass_up, 0)

    inner = (z > 0) & (z < top)

    @pl.when(inner & (2 * z < top))
    def _():
        all_up()
        all_down()

    @pl.when(inner & (2 * z >= top))
    def _():
        all_down()
        all_up()

    summed = small[...]
    for k in range(1, nodes_n):
        small_copy(k).wait_recv()
        summed = summed + small_in[k - 1]
    spec_out[...] = summed
    for k in range(1, tm_n):
        spec_copy(k).start()
    gtime_ref[...] = summed[:, :steps] * scale_time

    def finish(c, _):
        g = z * per + c

        @pl.when(z < top)
        def _():
            sum_copy(g, False).wait_recv()
            mine[g] += above[g].astype(F32)

        @pl.when(z > 0)
        def _():
            sum_copy(g, True).wait_recv()
            mine[g] += below[g].astype(F32)

        return 0

    lax.fori_loop(0, per, finish, 0)
    for c in range(per):
        gnode_ref[:, c * width:(c + 1) * width] = mine[z * per + c] * scale_node

    for k in range(1, tm_n):
        spec_copy(k).wait_recv()
        summed = summed + spec_in[k - 1]
    gspec_ref[...] = summed[:, steps:steps + species] * scale_spec

    def drain(p, _):
        owner, g = place(p)

        @pl.when((owner <= z) & (z < top))
        def _():
            gather_copy(g, True).wait_send()

        @pl.when((owner >= z) & (z > 0))
        def _():
            gather_copy(g, False).wait_send()

        @pl.when(owner > z)
        def _():
            sum_copy(g, True).wait_send()

        @pl.when(owner < z)
        def _():
            sum_copy(g, False).wait_send()

        return 0

    lax.fori_loop(0, total, drain, 0)
    for k in range(1, nodes_n):
        small_copy(k).wait_send()
    for k in range(1, tm_n):
        spec_copy(k).wait_send()


def shards(nodes_n, tm_n, observed, node_factor, time_factor, species_factor):
    rank, own = node_factor.shape
    rows, flat = observed.shape
    steps, species = time_factor.shape[1], species_factor.shape[1]
    width = min(own, 256)
    total = rows // width
    lanes = 128 * ((steps + species + 127) // 128)
    nodes_all, steps_all = rows * nodes_n, steps * tm_n
    scales = (
        1.0 / math.sqrt(steps_all * species),
        1.0 / math.sqrt(nodes_all * species),
        1.0 / math.sqrt(nodes_all * steps_all),
    )
    vmem = pl.BlockSpec(memory_space=pltpu.VMEM)
    dma = pltpu.SemaphoreType.DMA
    return pl.pallas_call(
        functools.partial(kernel, nodes_n, tm_n, width, scales),
        out_shape=(
            jax.ShapeDtypeStruct((rank, own), F32),
            jax.ShapeDtypeStruct((rank, steps), F32),
            jax.ShapeDtypeStruct((rank, species), F32),
        ),
        in_specs=[pl.BlockSpec(memory_space=pl.ANY), vmem, vmem, vmem],
        out_specs=(vmem, vmem, vmem),
        scratch_shapes=[
            pltpu.VMEM((rows, flat), BF16),
            pltpu.VMEM((total, rank, width), BF16),
            pltpu.VMEM((total, rank, width), F32),
            pltpu.VMEM((total, rank, width), LINK),
            pltpu.VMEM((total, rank, width), LINK),
            pltpu.VMEM((total, rank, width), LINK),
            pltpu.VMEM((rank, flat), BF16),
            pltpu.VMEM((rank, flat), F32),
            pltpu.VMEM((rank, flat), F32),
            pltpu.VMEM((rank, flat), F32),
            pltpu.VMEM((rank, lanes), F32),
            pltpu.VMEM((nodes_n - 1, rank, lanes), F32),
            pltpu.VMEM((rank, lanes), F32),
            pltpu.VMEM((tm_n - 1, rank, lanes), F32),
            dma((total,)),
            dma((2, total)),
            dma((total,)),
            dma((total,)),
            dma((total,)),
            dma((total,)),
            dma((nodes_n - 1,)),
            dma((nodes_n - 1,)),
            dma((tm_n - 1,)),
            dma((tm_n - 1,)),
        ],
        compiler_params=pltpu.CompilerParams(
            collective_id=0, has_side_effects=True, vmem_limit_bytes=48 * 1024 * 1024
        ),
        cost_estimate=pl.CostEstimate(
            flops=6 * rows * flat * rank, bytes_accessed=2 * rows * flat, transcendentals=0
        ),
    )(observed, node_factor, time_factor, species_factor)


def solution(mesh):
    in_specs = (P("node", "tm"), P(None, ("node", "tm")), P(None, "tm"), P())
    out_specs = (P(None, ("node", "tm")), P(None, "tm"), P())
    body = functools.partial(shards, mesh.shape["node"], mesh.shape["tm"])
    return jax.shard_map(body, mesh=mesh, in_specs=in_specs, out_specs=out_specs, check_vma=False)
```

time: 130 us -> 49.8 us (0.38)
  blocking collectives: 82.1 us -> 0 us
  Pallas kernels: 0 us -> 44.5 us
  matrix products: 14 us -> 0 us
  between operations: 14.1 us -> 0.64 us
  local copies, waits for them, and re-layouts: 15.3 us -> 4.39 us
  other arithmetic: 3.76 us -> 0 us
    psum x2 -> x0, blocking collectives: 64.6 us -> none  [the longest x1 41.5 us: shards(): species_grad = lax.psum(species_grad, ('node', 'tm'))]
    pallas_call x0 -> x1, Pallas kernels: none -> 44.5 us  [shards(): pl.pallas_call(functools.partial(kernel, nodes_n, tm_n, width, scales), o...]
    all_gather x1 -> x0, blocking collectives: 17.6 us -> none  [shards(): lax.all_gather(node_factor, 'tm', axis=1, tiled=True).astype(jnp.float32)]
    dot_general x3 -> x0, matrix products: 14 us -> none  [the longest x1 5.7 us: shards(): lax.dot_general(derivative_wide, factor_wide, (((0,), (1,)), ((), ())), p...]
    unnamed x3 -> x7, local copies, waits for them, and re-layouts: 14.5 us -> 3.72 us
    div x3 -> x0, other arithmetic: 2.89 us -> none  [the longest x1 1.67 us: shards(): grad_node = grad_node / math.sqrt(steps_all * species)]
  transfers between devices with their start and end apart: 1 -> 0, of which waited for: 0 -> 0; matrix products, arithmetic and copies ran while one was open for 5% -> 0% of each run, Pallas kernels for 0% -> 0%
where the time goes in v1:
time: 49.8 us; the launch traced here: 49.5 us
  Pallas kernels  44.5 us (89%)
  local copies, waits for them, and re-layouts  4.39 us (9%)
  between operations  0.64 us (1%)
    pallas_call x1, Pallas kernels, shards(): pl.pallas_call(functools.partial(kernel, nodes_n, tm_n, width, scales), o...  44.5 us
    unnamed x7, local copies, waits for them, and re-layouts  3.72 us

profile of v1, /device:TPU:0, one launch (start us, length us, event | category | flops | bytes accessed | tf_op | source)
XLA Modules:
  0.0 49.5 jit_solution(16794154928285987659)
XLA Ops:
  0.6 0.8 %copy.7.sf_ref = bf16[64,16]{1,0:T(8,128)(2,1)S(1)} copy(bf16[64,16]{0,1:T(8,128)(2,1)} %param.7) | data formatting | bytes 4096 | tf_op args[3]
  1.4 0.0 copy-start
  1.4 0.9 %copy-done = bf16[64,1024]{1,0:T(8,128)(2,1)S(1)} copy-done((bf16[64,1024]{1,0:T(8,128)(2,1)S(1)}, bf16[64,1024]{1,0:T(8,128)(2,1)}, u32[]{:S(2)}) %copy-start) | copy-done | bytes 131096
  2.3 0.0 copy-start.1
  2.3 0.7 %copy-done.1 = bf16[64,64]{1,0:T(8,128)(2,1)S(1)} copy-done((bf16[64,64]{1,0:T(8,128)(2,1)S(1)}, bf16[64,64]{1,0:T(8,128)(2,1)}, u32[]{:S(2)}) %copy-start.1) | copy-done | bytes 8216
  3.0 44.5 %shard_map.67 = (f32[64,1024]{1,0:T(8,128)S(1)}, f32[64,64]{1,0:T(8,128)S(1)}, f32[64,16]{1,0:T(8,128)S(1)}) custom-call(bf16[4096,1024]{1,0:T(8,128)(2,1)} %obs_ref.1, bf16[64,1024]{1,0:T(8,128)(2,1)S(1)} %copy-done, bf16[64,64]{1,0:T(8,128)(2,1)S(1)} %copy-done.1, bf16[64,16]{1,0:T(8,128)(2,1)S(1)} %copy.7.sf_ref), custom_call_target="tpu_custom_call" | custom-call | flops 1610612736 | bytes 8388608 | tf_op jit(solution)/shard_map/pallas_call | solution.py:312
  47.5 0.7 %copy.8 = f32[64,16]{0,1:T(8,128)} copy(f32[64,16]{1,0:T(8,128)S(1)} %get-tuple-element.5) | data formatting | bytes 8192 | tf_op jit(solution)/shard_map/pallas_call | solution.py:312
  48.2 0.7 %copy.11 = f32[64,1024]{1,0:T(8,128)} copy(f32[64,1024]{1,0:T(8,128)S(1)} %get-tuple-element.9) | data formatting | bytes 524288
  48.9 0.6 %copy.12 = f32[64,64]{1,0:T(8,128)} copy(f32[64,64]{1,0:T(8,128)S(1)} %get-tuple-element.10) | data formatting | bytes 32768
Async XLA Ops:
  1.4 0.9 %copy-start = (bf16[64,1024]{1,0:T(8,128)(2,1)S(1)}, bf16[64,1024]{1,0:T(8,128)(2,1)}, u32[]{:S(2)}) copy-start(bf16[64,1024]{1,0:T(8,128)(2,1)} %nf_ref.1) | copy-start | bytes 393220
  2.3 0.7 %copy-start.1 = (bf16[64,64]{1,0:T(8,128)(2,1)S(1)}, bf16[64,64]{1,0:T(8,128)(2,1)}, u32[]{:S(2)}) copy-start(bf16[64,64]{1,0:T(8,128)(2,1)} %tf_ref.1) | copy-start | bytes 24580

commit v2 on v1

--- a/solution.py
+++ b/solution.py
@@ -11,16 +11,15 @@
 MESH = pl.DeviceIdType.MESH
 F32 = jnp.float32
 BF16 = jnp.bfloat16
-LINK = jnp.float32
 LOOK = 2
-COLS = 256
+COLS = 1024
 
 
 def kernel(
     nodes_n, tm_n, width, scales,
     obs_ref, nf_ref, tf_ref, sf_ref,
     gnode_ref, gtime_ref, gspec_ref,
-    obs_v, gath, mine, out, above, below, khatri, spread_t, spread_s, ctot,
+    obs_v, gath, mine, out, above, below, out_w, above_w, below_w, khatri, spread_t, spread_s, ctot,
     small, small_in, spec_out, spec_in,
     obs_sem, g_send, g_recv, r_send, a_recv, b_recv, s_send, s_recv, p_send, p_recv,
 ):
@@ -65,12 +64,50 @@
             device_id={"tm": z + 1 if up else z - 1}, device_id_type=MESH,
         )
 
-    def sum_copy(g, up):
+    def sum_copy(g, up, wide):
+        source = out_w if wide else out
+        target = (below_w if up else above_w) if wide else (below if up else above)
         return pltpu.make_async_remote_copy(
-            src_ref=out.at[g], dst_ref=(below if up else above).at[g],
+            src_ref=source.at[g], dst_ref=target.at[g],
             send_sem=r_send.at[g], recv_sem=(b_recv if up else a_recv).at[g],
             device_id={"tm": z + 1 if up else z - 1}, device_id_type=MESH,
         )
+
+    def by_type(terms, act):
+        if tm_n <= 3:
+            act(False)
+            return
+
+        @pl.when(terms >= 3)
+        def _():
+            act(True)
+
+        @pl.when(terms < 3)
+        def _():
+            act(False)
+
+    def send_sum(g, up, value):
+        def act(wide):
+            if wide:
+                out_w[g] = value
+            else:
+                out[g] = value.astype(BF16)
+            sum_copy(g, up, wide).start()
+
+        by_type(z + 1 if up else tm_n - z, act)
+
+    def take_sum(g, up):
+        def act(wide):
+            sum_copy(g, up, wide).wait_recv()
+            if wide:
+                mine[g] += (below_w if up else above_w)[g]
+            else:
+                mine[g] += (below if up else above)[g].astype(F32)
+
+        by_type(z if up else top - z, act)
+
+    def sent_sum(g, up):
+        by_type(z + 1 if up else tm_n - z, lambda wide: sum_copy(g, up, wide).wait_send())
 
     def small_copy(k):
         return pltpu.make_async_remote_copy(
@@ -170,13 +207,11 @@
 
         @pl.when((z == top) & (owner < z))
         def _():
-            out[g] = part.astype(out.dtype)
-            sum_copy(g, False).start()
+            send_sum(g, False, part)
 
         @pl.when((z == 0) & (owner > z))
         def _():
-            out[g] = part.astype(out.dtype)
-            sum_copy(g, True).start()
+            send_sum(g, True, part)
 
         return 0
 
@@ -200,15 +235,13 @@
         small_copy(k).start()
 
     def pass_up(g, _):
-        sum_copy(g, True).wait_recv()
-        out[g] = (mine[g] + below[g].astype(F32)).astype(out.dtype)
-        sum_copy(g, True).start()
+        take_sum(g, True)
+        send_sum(g, True, mine[g])
         return 0
 
     def pass_down(g, _):
-        sum_copy(g, False).wait_recv()
-        out[g] = (mine[g] + above[g].astype(F32)).astype(out.dtype)
-        sum_copy(g, False).start()
+        take_sum(g, False)
+        send_sum(g, False, mine[g])
         return 0
 
     def all_down():
@@ -247,13 +280,11 @@
 
         @pl.when(z < top)
         def _():
-            sum_copy(g, False).wait_recv()
-            mine[g] += above[g].astype(F32)
+            take_sum(g, False)
 
         @pl.when(z > 0)
         def _():
-            sum_copy(g, True).wait_recv()
-            mine[g] += below[g].astype(F32)
+            take_sum(g, True)
 
         return 0
 
@@ -279,11 +310,11 @@
 
         @pl.when(owner > z)
         def _():
-            sum_copy(g, True).wait_send()
+            sent_sum(g, True)
 
         @pl.when(owner < z)
         def _():
-            sum_copy(g, False).wait_send()
+            sent_sum(g, False)
 
         return 0
 
@@ -322,9 +353,12 @@
             pltpu.VMEM((rows, flat), BF16),
             pltpu.VMEM((total, rank, width), BF16),
             pltpu.VMEM((total, rank, width), F32),
-            pltpu.VMEM((total, rank, width), LINK),
-            pltpu.VMEM((total, rank, width), LINK),
-            pltpu.VMEM((total, rank, width), LINK),
+            pltpu.VMEM((total, rank, width), BF16),
+            pltpu.VMEM((total, rank, width), BF16),
+            pltpu.VMEM((total, rank, width), BF16),
+            pltpu.VMEM((total, rank, width), F32),
+            pltpu.VMEM((total, rank, width), F32),
+            pltpu.VMEM((total, rank, width), F32),
             pltpu.VMEM((rank, flat), BF16),
             pltpu.VMEM((rank, flat), F32),
             pltpu.VMEM((rank, flat), F32),

time: 49.8 us -> 38.9 us (0.78)
  Pallas kernels: 44.5 us -> 33.6 us
    pallas_call x1, Pallas kernels: 44.5 us -> 33.6 us  [shards(): pl.pallas_call(functools.partial(kernel, nodes_n, tm_n, width, scales), o...]
where the time goes in v2:
time: 38.9 us; the launch traced here: 38.6 us
  Pallas kernels  33.6 us (86%)
  local copies, waits for them, and re-layouts  4.39 us (11%)
  between operations  0.64 us (2%)
    pallas_call x1, Pallas kernels, shards(): pl.pallas_call(functools.partial(kernel, nodes_n, tm_n, width, scales), o...  33.6 us
    unnamed x7, local copies, waits for them, and re-layouts  3.72 us

profile of v2, /device:TPU:0, one launch (start us, length us, event | category | flops | bytes accessed | tf_op | source)
XLA Modules:
  0.0 38.6 jit_solution(1684318891800586869)
XLA Ops:
  0.6 0.8 %copy.7.sf_ref = bf16[64,16]{1,0:T(8,128)(2,1)S(1)} copy(bf16[64,16]{0,1:T(8,128)(2,1)} %param.7) | data formatting | bytes 4096 | tf_op args[3]
  1.4 0.0 copy-start
  1.4 0.9 %copy-done = bf16[64,1024]{1,0:T(8,128)(2,1)S(1)} copy-done((bf16[64,1024]{1,0:T(8,128)(2,1)S(1)}, bf16[64,1024]{1,0:T(8,128)(2,1)}, u32[]{:S(2)}) %copy-start) | copy-done | bytes 131096
  2.3 0.0 copy-start.1
  2.3 0.7 %copy-done.1 = bf16[64,64]{1,0:T(8,128)(2,1)S(1)} copy-done((bf16[64,64]{1,0:T(8,128)(2,1)S(1)}, bf16[64,64]{1,0:T(8,128)(2,1)}, u32[]{:S(2)}) %copy-start.1) | copy-done | bytes 8216
  3.0 33.6 %shard_map.67 = (f32[64,1024]{1,0:T(8,128)S(1)}, f32[64,64]{1,0:T(8,128)S(1)}, f32[64,16]{1,0:T(8,128)S(1)}) custom-call(bf16[4096,1024]{1,0:T(8,128)(2,1)} %obs_ref.1, bf16[64,1024]{1,0:T(8,128)(2,1)S(1)} %copy-done, bf16[64,64]{1,0:T(8,128)(2,1)S(1)} %copy-done.1, bf16[64,16]{1,0:T(8,128)(2,1)S(1)} %copy.7.sf_ref), custom_call_target="tpu_custom_call" | custom-call | flops 1610612736 | bytes 8388608 | tf_op jit(solution)/shard_map/pallas_call | solution.py:343
  36.6 0.7 %copy.8 = f32[64,16]{0,1:T(8,128)} copy(f32[64,16]{1,0:T(8,128)S(1)} %get-tuple-element.5) | data formatting | bytes 8192 | tf_op jit(solution)/shard_map/pallas_call | solution.py:343
  37.3 0.7 %copy.11 = f32[64,1024]{1,0:T(8,128)} copy(f32[64,1024]{1,0:T(8,128)S(1)} %get-tuple-element.9) | data formatting | bytes 524288
  38.0 0.6 %copy.12 = f32[64,64]{1,0:T(8,128)} copy(f32[64,64]{1,0:T(8,128)S(1)} %get-tuple-element.10) | data formatting | bytes 32768
Async XLA Ops:
  1.4 0.9 %copy-start = (bf16[64,1024]{1,0:T(8,128)(2,1)S(1)}, bf16[64,1024]{1,0:T(8,128)(2,1)}, u32[]{:S(2)}) copy-start(bf16[64,1024]{1,0:T(8,128)(2,1)} %nf_ref.1) | copy-start | bytes 393220
  2.3 0.7 %copy-start.1 = (bf16[64,64]{1,0:T(8,128)(2,1)S(1)}, bf16[64,64]{1,0:T(8,128)(2,1)}, u32[]{:S(2)}) copy-start(bf16[64,64]{1,0:T(8,128)(2,1)} %tf_ref.1) | copy-start | bytes 24580

commit v3 on v2

--- a/solution.py
+++ b/solution.py
@@ -17,22 +17,24 @@
 
 def kernel(
     nodes_n, tm_n, width, scales,
-    obs_ref, nf_ref, tf_ref, sf_ref,
+    obs_ref, nf_ref, tf_hbm, sf_hbm,
     gnode_ref, gtime_ref, gspec_ref,
-    obs_v, gath, mine, out, above, below, out_w, above_w, below_w, khatri, spread_t, spread_s, ctot,
+    obs_v, gath, mine, out, above, below, out_w, above_w, below_w, khatri, spread_t, spread_s, ctot, wide, tf_ref, sf_ref,
     small, small_in, spec_out, spec_in,
-    obs_sem, g_send, g_recv, r_send, a_recv, b_recv, s_send, s_recv, p_send, p_recv,
+    obs_sem, g_send, g_recv, r_send, a_recv, b_recv, s_send, s_recv, p_send, p_recv, nf_sem, f_sem,
 ):
     rank, own = nf_ref.shape
     rows, flat = obs_ref.shape
     steps = tf_ref.shape[1]
-    species = sf_ref.shape[1]
+    species = sf_ref.shape[0]
     per = own // width
     total = tm_n * per
-    lanes = small.shape[1]
     z = lax.axis_index("tm")
     me = lax.axis_index("node")
     top = tm_n - 1
+    inner = (z > 0) & (z < top)
+    low_half = 2 * z < top
+    early = tm_n <= 4
     scale_node, scale_time, scale_spec = scales
 
     def place(p):
@@ -132,9 +134,35 @@
         pl.semaphore_signal(
             barrier, inc=1, device_id={"tm": lax.rem(z + k, tm_n)}, device_id_type=MESH
         )
+    time_copy = pltpu.make_async_copy(tf_hbm, tf_ref, f_sem.at[0])
+    species_copy = pltpu.make_async_copy(sf_hbm, sf_ref, f_sem.at[1])
+    time_copy.start()
+    species_copy.start()
+    own_copies = [
+        pltpu.make_async_copy(
+            nf_ref.at[:, c * width:(c + 1) * width], gath.at[z * per + c], nf_sem.at[c]
+        )
+        for c in range(per)
+    ]
+    for copy in own_copies:
+        copy.start()
     lax.fori_loop(0, total, start_obs, 0)
-    for c in range(per):
-        gath[z * per + c] = nf_ref[:, c * width:(c + 1) * width]
+    col = lax.broadcasted_iota(jnp.int32, (steps, flat), 1)
+    row = lax.broadcasted_iota(jnp.int32, (steps, flat), 0) * species
+    wide[:steps, :] = jnp.where((col >= row) & (col < row + species), 1.0, 0.0).astype(BF16)
+    col_s = lax.rem(lax.broadcasted_iota(jnp.int32, (species, flat), 1), species)
+    row_s = lax.broadcasted_iota(jnp.int32, (species, flat), 0)
+    wide[steps:, :] = jnp.where(col_s == row_s, 1.0, 0.0).astype(BF16)
+    time_copy.wait()
+    species_copy.wait()
+    spread_t[...] = jnp.dot(tf_ref[...], wide[:steps, :], preferred_element_type=F32)
+    spread_s[...] = lax.dot_general(
+        sf_ref[...], wide[steps:, :], (((0,), (0,)), ((), ())), preferred_element_type=F32
+    )
+    khatri[...] = (spread_t[...] * spread_s[...]).astype(BF16)
+    ctot[...] = jnp.zeros_like(ctot)
+    for copy in own_copies:
+        copy.wait()
     pl.semaphore_wait(barrier, nodes_n - 1 + tm_n - 1)
 
     def start_gather(c, _):
@@ -151,17 +179,6 @@
         return 0
 
     lax.fori_loop(0, per, start_gather, 0)
-
-    col = lax.broadcasted_iota(jnp.int32, (steps, flat), 1)
-    row = lax.broadcasted_iota(jnp.int32, (steps, flat), 0) * species
-    wide_t = jnp.where((col >= row) & (col < row + species), 1.0, 0.0).astype(BF16)
-    col_s = lax.rem(lax.broadcasted_iota(jnp.int32, (species, flat), 1), species)
-    row_s = lax.broadcasted_iota(jnp.int32, (species, flat), 0)
-    wide_s = jnp.where(col_s == row_s, 1.0, 0.0).astype(BF16)
-    spread_t[...] = jnp.dot(tf_ref[...], wide_t, preferred_element_type=F32)
-    spread_s[...] = jnp.dot(sf_ref[...], wide_s, preferred_element_type=F32)
-    khatri[...] = (spread_t[...] * spread_s[...]).astype(BF16)
-    ctot[...] = jnp.zeros_like(ctot)
 
     def relay(p):
         owner, g = place(p)
@@ -196,6 +213,16 @@
             ctot[:, c:c + COLS] += jnp.dot(factor, derivative, preferred_element_type=F32)
         return part
 
+    def pass_up(g, _):
+        take_sum(g, True)
+        send_sum(g, True, mine[g])
+        return 0
+
+    def pass_down(g, _):
+        take_sum(g, False)
+        send_sum(g, False, mine[g])
+        return 0
+
     def step(p, _):
         @pl.when(p + LOOK < total)
         def _():
@@ -213,67 +240,67 @@
         def _():
             send_sum(g, True, part)
 
+        if early:
+            @pl.when((p >= total - per) & inner & low_half)
+            def _():
+                pass_up((z + 1) * per + p - (total - per), 0)
+
+            @pl.when((p >= total - per) & inner & jnp.logical_not(low_half))
+            def _():
+                pass_down((z - 1) * per + p - (total - per), 0)
+
         return 0
 
     for p in range(LOOK):
         relay(p)
     lax.fori_loop(0, total, step, 0)
 
-    time_col = lax.broadcasted_iota(jnp.int32, (flat, lanes), 1)
-    time_row = lax.broadcasted_iota(jnp.int32, (flat, lanes), 0)
-    at_step = time_col * species
-    pick_t = jnp.where((time_row >= at_step) & (time_row < at_step + species), 1.0, 0.0)
-    pick_s = jnp.where(lax.rem(time_row, species) == time_col - steps, 1.0, 0.0)
-    small[...] = jnp.dot(
-        ctot[...] * spread_s[...], pick_t, precision=lax.Precision.HIGHEST,
-        preferred_element_type=F32,
-    ) + jnp.dot(
-        ctot[...] * spread_t[...], pick_s, precision=lax.Precision.HIGHEST,
-        preferred_element_type=F32,
-    )
+    def fold(pick, values):
+        result = jnp.zeros((pick.shape[0], rank), F32)
+        for _ in range(3):
+            term = values.astype(BF16)
+            values = values - term.astype(F32)
+            result = result + lax.dot_general(
+                pick, term, (((1,), (1,)), ((), ())), preferred_element_type=F32
+            )
+        return result
+
+    small[:steps, :] = fold(wide[:steps, :], ctot[...] * spread_s[...])
+    small[steps:, :] = fold(wide[steps:, :], ctot[...] * spread_t[...])
     for k in range(1, nodes_n):
         small_copy(k).start()
 
-    def pass_up(g, _):
-        take_sum(g, True)
-        send_sum(g, True, mine[g])
-        return 0
-
-    def pass_down(g, _):
-        take_sum(g, False)
-        send_sum(g, False, mine[g])
-        return 0
-
-    def all_down():
+    def all_down(skip):
         def owner_down(i, _):
             first = (z - 1 - i) * per
             return lax.fori_loop(first, first + per, pass_down, 0)
 
-        lax.fori_loop(0, z, owner_down, 0)
-
-    def all_up():
-        lax.fori_loop((z + 1) * per, total, pass_up, 0)
-
-    inner = (z > 0) & (z < top)
-
-    @pl.when(inner & (2 * z < top))
+        lax.fori_loop(skip, z, owner_down, 0)
+
+    def all_up(skip):
+        lax.fori_loop((z + 1 + skip) * per, total, pass_up, 0)
+
+    done = 1 if early else 0
+
+    @pl.when(inner & low_half)
     def _():
-        all_up()
-        all_down()
-
-    @pl.when(inner & (2 * z >= top))
+        all_up(done)
+        all_down(0)
+
+    @pl.when(inner & jnp.logical_not(low_half))
     def _():
-        all_down()
-        all_up()
+        all_down(done)
+        all_up(0)
 
     summed = small[...]
     for k in range(1, nodes_n):
         small_copy(k).wait_recv()
         summed = summed + small_in[k - 1]
-    spec_out[...] = summed
+    spec_out[...] = summed[steps:, :]
+    spec_sum = summed[steps:, :]
     for k in range(1, tm_n):
         spec_copy(k).start()
-    gtime_ref[...] = summed[:, :steps] * scale_time
+    gtime_ref[...] = summed[:steps, :].T * scale_time
 
     def finish(c, _):
         g = z * per + c
@@ -294,8 +321,8 @@
 
     for k in range(1, tm_n):
         spec_copy(k).wait_recv()
-        summed = summed + spec_in[k - 1]
-    gspec_ref[...] = summed[:, steps:steps + species] * scale_spec
+        spec_sum = spec_sum + spec_in[k - 1]
+    gspec_ref[...] = spec_sum * scale_spec
 
     def drain(p, _):
         owner, g = place(p)
@@ -331,7 +358,7 @@
     steps, species = time_factor.shape[1], species_factor.shape[1]
     width = min(own, 256)
     total = rows // width
-    lanes = 128 * ((steps + species + 127) // 128)
+    both = steps + species
     nodes_all, steps_all = rows * nodes_n, steps * tm_n
     scales = (
         1.0 / math.sqrt(steps_all * species),
@@ -340,14 +367,15 @@
     )
     vmem = pl.BlockSpec(memory_space=pltpu.VMEM)
     dma = pltpu.SemaphoreType.DMA
-    return pl.pallas_call(
+    anywhere = pl.BlockSpec(memory_space=pl.ANY)
+    grad_node, grad_time, grad_species = pl.pallas_call(
         functools.partial(kernel, nodes_n, tm_n, width, scales),
         out_shape=(
             jax.ShapeDtypeStruct((rank, own), F32),
             jax.ShapeDtypeStruct((rank, steps), F32),
-            jax.ShapeDtypeStruct((rank, species), F32),
+            jax.ShapeDtypeStruct((species, rank), F32),
         ),
-        in_specs=[pl.BlockSpec(memory_space=pl.ANY), vmem, vmem, vmem],
+        in_specs=[anywhere] * 4,
         out_specs=(vmem, vmem, vmem),
         scratch_shapes=[
             pltpu.VMEM((rows, flat), BF16),
@@ -363,10 +391,13 @@
             pltpu.VMEM((rank, flat), F32),
             pltpu.VMEM((rank, flat), F32),
             pltpu.VMEM((rank, flat), F32),
-            pltpu.VMEM((rank, lanes), F32),
-            pltpu.VMEM((nodes_n - 1, rank, lanes), F32),
-            pltpu.VMEM((rank, lanes), F32),
-            pltpu.VMEM((tm_n - 1, rank, lanes), F32),
+            pltpu.VMEM((both, flat), BF16),
+            pltpu.VMEM((rank, steps), BF16),
+            pltpu.VMEM((species, rank), BF16),
+            pltpu.VMEM((both, rank), F32),
+            pltpu.VMEM((nodes_n - 1, both, rank), F32),
+            pltpu.VMEM((species, rank), F32),
+            pltpu.VMEM((tm_n - 1, species, rank), F32),
             dma((total,)),
             dma((2, total)),
             dma((total,)),
@@ -377,14 +408,17 @@
             dma((nodes_n - 1,)),
             dma((tm_n - 1,)),
             dma((tm_n - 1,)),
+            dma((own // width,)),
+            dma((2,)),
         ],
         compiler_params=pltpu.CompilerParams(
-            collective_id=0, has_side_effects=True, vmem_limit_bytes=48 * 1024 * 1024
+            collective_id=0, has_side_effects=True, vmem_limit_bytes=56 * 1024 * 1024
         ),
         cost_estimate=pl.CostEstimate(
             flops=6 * rows * flat * rank, bytes_accessed=2 * rows * flat, transcendentals=0
         ),
-    )(observed, node_factor, time_factor, species_factor)
+    )(observed, node_factor, time_factor, species_factor.T)
+    return grad_node, grad_time, grad_species.T
 
 
 def solution(mesh):

time: 38.9 us -> 39.9 us (1.026)
  Pallas kernels: 33.6 us -> 34.6 us
    pallas_call x1, Pallas kernels: 33.6 us -> 34.6 us  [shards(): pl.pallas_call(functools.partial(kernel, nodes_n, tm_n, width, scales), o...]
    pallas_call x1 -> x0, local copies, waits for them, and re-layouts: 0.67 us -> none  [shards(): pl.pallas_call(functools.partial(kernel, nodes_n, tm_n, width, scales), o...]
    unnamed x7 -> x3, local copies, waits for them, and re-layouts: 3.72 us -> 4.34 us
where the time goes in v3:
time: 39.9 us; the launch traced here: 39.6 us
  Pallas kernels  34.6 us (87%)
  local copies, waits for them, and re-layouts  4.34 us (11%)
  between operations  0.64 us (2%)
    pallas_call x1, Pallas kernels, shards(): pl.pallas_call(functools.partial(kernel, nodes_n, tm_n, width, scales), o...  34.6 us
    unnamed x3, local copies, waits for them, and re-layouts  4.34 us

profile of v3, /device:TPU:0, one launch (start us, length us, event | category | flops | bytes accessed | tf_op | source)
XLA Modules:
  0.0 39.6 jit_solution(4495183244520603632)
XLA Ops:
  0.6 34.6 %shard_map.67 = (f32[64,1024]{1,0:T(8,128)}, f32[64,64]{1,0:T(8,128)}, f32[16,64]{1,0:T(8,128)}) custom-call(bf16[4096,1024]{1,0:T(8,128)(2,1)} %obs_ref.1, bf16[64,1024]{1,0:T(8,128)(2,1)} %nf_ref.1, bf16[64,64]{1,0:T(8,128)(2,1)} %tf_hbm.1, bf16[16,64]{1,0:T(8,128)(2,1)} %bitcast.3), custom_call_target="tpu_custom_call" | custom-call | flops 1610612736 | bytes 8388608 | tf_op jit(solution)/shard_map/pallas_call | solution.py:371
  35.3 1.7 %copy.10 = f32[64,1024]{1,0:T(8,128)} copy(f32[64,1024]{1,0:T(8,128)} %get-tuple-element.12) | data formatting | bytes 524288
  36.9 1.4 %copy.11 = f32[64,64]{1,0:T(8,128)} copy(f32[64,64]{1,0:T(8,128)} %get-tuple-element.13) | data formatting | bytes 32768
  38.3 1.3 %copy.12 = f32[64,16]{0,1:T(8,128)} copy(f32[64,16]{0,1:T(8,128)} %bitcast.2) | data formatting | bytes 8192
